TPU v7x, 32 devices: a whole 2x2x4 slice. The times are simulated.
32 devices in a mesh: dp: 16 (over z, x, core), tensor: 2 (over y).
Axes of the slice: x: 2, y: 2, z: 4, core: 2. Of those that a mesh axis runs over, the one named last changes fastest.
Arguments:
- layer_in: bfloat16 [16, 2, 1024, 768], P(None, 'tensor', 'dp'), may hold values from -6 to 6
- out_grad: bfloat16 [16, 2, 1024, 768], P(None, 'tensor', 'dp'), may hold values from -6 to 6
- seq_lengths: int32 [16], replicated, may hold values from 1 to 2048, 20480 in all
- slot_perm: int32 [16], replicated, may hold values from 0 to 15, each once
- norm_gain: float32 [768], replicated, may hold values from 0.1 to 1.9
- w_gate: bfloat16 [768, 1536], P('dp', 'tensor'), may hold values from -0.21875 to 0.21875
- w_inner: bfloat16 [768, 1536], P('dp', 'tensor'), may hold values from -0.21875 to 0.21875
- w_bc: bfloat16 [768, 128], P('dp'), may hold values from -0.21875 to 0.21875
- w_dt: bfloat16 [768, 48], P('dp', 'tensor'), may hold values from -0.21875 to 0.21875
- conv_x: float32 [4, 1536], P(None, 'tensor'), may hold values from -3 to 3
- conv_bc: float32 [4, 128], replicated, may hold values from -2 to 2
- dt_bias: float32 [48], P('tensor'), may hold values from -4 to -2
- a_log: float32 [24], P('tensor'), may hold values from -4.5 to 0.5
- dskip: float32 [24], P('tensor'), may hold values from 1 to 3
- inner_gain: float32 [1536], P('tensor'), may hold values from 0.1 to 1.9
- w_out: bfloat16 [1536, 768], P('tensor', 'dp'), may hold values from -0.15625 to 0.15625
Outputs:
- output: bfloat16 [16, 2, 1024, 768], P(None, 'tensor', 'dp')
- input_grad: bfloat16 [16, 2, 1024, 768], P(None, 'tensor', 'dp')
- grad_norm_gain: float32 [768], replicated
- grad_w_gate: float32 [768, 1536], P('dp', 'tensor')
- grad_w_inner: float32 [768, 1536], P('dp', 'tensor')
- grad_w_bc: float32 [768, 128], P('dp')
- grad_w_dt: float32 [768, 48], P('dp', 'tensor')
- grad_conv_x: float32 [4, 1536], P(None, 'tensor')
- grad_conv_bc: float32 [4, 128], replicated
- grad_dt_bias: float32 [48], P('tensor')
- grad_a_log: float32 [24], P('tensor')
- grad_dskip: float32 [24], P('tensor')
- grad_inner_gain: float32 [1536], P('tensor')
- grad_w_out: float32 [1536, 768], P('tensor', 'dp')
Inputs may be any that keep to these rules, and one draw needn't show every extreme that they name: Sequence s is computed in slot slot_perm[s]; slot i belongs to index i of dp; out_grad, output and input_grad are indexed by slot. `seq_lengths`: some sequence has exactly 2048 valid positions.
All inputs are finite; a program needn't handle non-finite values.
Results may differ from a plain program's by a relative error of at most 0.011.
Values may be sent and summed in bfloat16 or wider, within the bound.
No kernel may reach another device: no remote copies, remote signals or barrier semaphores. Data moves between devices by JAX's collectives and lax.ppermute only.
A program may use at most 320 MiB of HBM per device.

v0:
```python
import jax
import jax.numpy as jnp
from jax import lax
from jax.sharding import PartitionSpec as P

BLOCK = 128
exact_prec = lax.Precision.HIGHEST


def causal_conv(values, kernel):
    taps_count = kernel.shape[0]
    length = values.shape[0]
    padded = jnp.pad(values, ((taps_count - 1, 0), (0, 0)))
    summed = jnp.zeros(values.shape, jnp.float32)
    for offset in range(taps_count):
        summed = summed + kernel[offset] * padded[offset : offset + length]
    return summed


def strict_scan(values, state_in, state_out, log_decay):
    length, head_count, head_width = values.shape
    blocks = length // BLOCK
    blocked = values.reshape(blocks, BLOCK, head_count, head_width)
    in_maps = state_in.reshape(blocks, BLOCK, -1)
    out_maps = state_out.reshape(blocks, BLOCK, -1)
    partial_sums = jnp.cumsum(log_decay.reshape(blocks, BLOCK, head_count), axis=1)
    scores = jnp.einsum("kin,kjn->kij", out_maps, in_maps, precision=exact_prec)
    row_ids = lax.broadcasted_iota(jnp.int32, (BLOCK, BLOCK), 0)
    col_ids = lax.broadcasted_iota(jnp.int32, (BLOCK, BLOCK), 1)
    lower = (row_ids > col_ids)[None, :, :, None]
    spread = partial_sums[:, :, None, :] - partial_sums[:, None, :, :]
    decay = jnp.where(lower, jnp.exp(jnp.where(lower, spread, 0.0)), 0.0)
    weights_in = scores[..., None] * decay
    inside = jnp.einsum("kijh,kjhp->kihp", weights_in, blocked, precision=exact_prec)
    to_end = jnp.exp(partial_sums[:, -1:, :] - partial_sums)
    block_states = jnp.einsum(
        "kjn,kjhp->khnp", in_maps, blocked * to_end[..., None], precision=exact_prec
    )
    block_decay = jnp.exp(partial_sums[:, -1, :])

    def carry_step(carried, item):
        decay_now, state_now = item
        return (carried * decay_now[:, None, None] + state_now, carried)

    start_state = jnp.zeros(block_states.shape[1:], jnp.float32)
    _, entering = lax.scan(carry_step, start_state, (block_decay, block_states))
    outside = jnp.einsum("kin,khnp->kihp", out_maps, entering, precision=exact_prec)
    outside = outside * jnp.exp(partial_sums)[..., None]
    return (inside + outside).reshape(length, head_count, head_width)


def mixer(
    inner_in, bc_raw, step_raw, gate, conv_x, conv_bc, dt_bias, a_log, dskip, inner_gain, mask
):
    length = inner_in.shape[0]
    head_count = a_log.shape[0]
    head_width = inner_in.shape[1] // head_count
    conv_out = jax.nn.silu(causal_conv(inner_in, conv_x))
    bc_conv = jax.nn.silu(causal_conv(bc_raw, conv_bc))
    state_width = bc_conv.shape[1] // 2
    state_in = bc_conv[:, :state_width]
    state_out = bc_conv[:, state_width:]
    step_size = jax.nn.softplus(step_raw + dt_bias).reshape(length, head_count, 2)
    log_decay = -step_size * jnp.exp(a_log)[None, :, None]
    heads_x = conv_out.reshape(length, head_count, head_width)
    forward_v = (mask[:, None] * step_size[:, :, 0])[:, :, None] * heads_x
    backward_v = (mask[:, None] * step_size[:, :, 1])[:, :, None] * heads_x
    forward_out = strict_scan(forward_v, state_in, state_out, log_decay[:, :, 0])
    backward_out = jnp.flip(
        strict_scan(
            jnp.flip(backward_v, 0),
            jnp.flip(state_in, 0),
            jnp.flip(state_out, 0),
            jnp.flip(log_decay[:, :, 1], 0),
        ),
        0,
    )
    mixture = forward_out + backward_out + dskip[None, :, None] * heads_x
    gated_out = mixture * jax.nn.silu(gate.reshape(length, head_count, head_width))
    scaled = gated_out * lax.rsqrt(jnp.mean(gated_out * gated_out, axis=-1, keepdims=True) + 1e-05)
    return (scaled * inner_gain.reshape(head_count, head_width)).reshape(
        length, head_count * head_width
    )


def project(left_operand, right_operand):
    return jnp.einsum(
        "web,bz->wez", left_operand, right_operand, preferred_element_type=jnp.float32
    )


def back_project(left_operand, right_operand):
    return jnp.einsum(
        "hkq,nq->hkn", left_operand, right_operand, preferred_element_type=jnp.float32
    )


def weight_grad(left_operand, right_operand):
    return jnp.einsum(
        "rno,rnm->om", left_operand, right_operand, preferred_element_type=jnp.float32
    )


def shards(
    layer_in,
    out_grad,
    seq_lengths,
    slot_perm,
    norm_gain,
    w_gate,
    w_inner,
    w_bc,
    w_dt,
    conv_x,
    conv_bc,
    dt_bias,
    a_log,
    dskip,
    inner_gain,
    w_out,
):
    dp_count = lax.axis_size("dp")
    rank_dp = lax.axis_index("dp")
    rank_tensor = lax.axis_index("tensor")
    seq_total = slot_perm.shape[0]
    seq_dev = seq_total // dp_count
    sender = jnp.argsort(slot_perm)
    placed_in = jnp.take(layer_in, sender, axis=0)
    local_in, local_grad = (
        lax.all_to_all(placed_in, "dp", split_axis=0, concat_axis=2, tiled=True),
        lax.all_to_all(out_grad, "dp", split_axis=0, concat_axis=2, tiled=True),
    )
    rows_half = local_in[:, 0].astype(jnp.float32)
    cot_half = local_grad[:, 0].astype(jnp.float32)
    half_len = rows_half.shape[1]
    full_len = half_len * lax.axis_size("tensor")
    mine = lax.dynamic_slice_in_dim(sender, rank_dp * seq_dev, seq_dev)
    my_lengths = jnp.take(seq_lengths, mine)
    positions = jnp.arange(full_len, dtype=jnp.int32)
    mask_full = (positions[None, :] < my_lengths[:, None]).astype(jnp.float32)
    mask_half = lax.dynamic_slice_in_dim(mask_full, rank_tensor * half_len, half_len, 1)
    inv_rms = lax.rsqrt(jnp.mean(rows_half * rows_half, axis=-1, keepdims=True) + 1e-05)
    unit_rows = rows_half * inv_rms
    normed_half = (unit_rows * norm_gain).astype(jnp.bfloat16)
    normed = lax.all_gather(normed_half, "tensor", axis=1, tiled=True)
    gate_w, inner_w, bc_w, dt_w, output_weight = (
        lax.all_gather(w_gate, "dp", axis=0, tiled=True),
        lax.all_gather(w_inner, "dp", axis=0, tiled=True),
        lax.all_gather(w_bc, "dp", axis=0, tiled=True),
        lax.all_gather(w_dt, "dp", axis=0, tiled=True),
        lax.all_gather(w_out, "dp", axis=1, tiled=True),
    )
    gate = project(normed, gate_w)
    inner_in = project(normed, inner_w)
    bc_raw = project(normed, bc_w)
    step_raw = project(normed, dt_w)

    def local_mixer(
        inner_val,
        bc_val,
        step_val,
        gate_val,
        convx_val,
        convbc_val,
        bias_val,
        alog_val,
        skip_val,
        gain_val,
    ):
        return jax.vmap(mixer, in_axes=(0, 0, 0, 0, None, None, None, None, None, None, 0))(
            inner_val,
            bc_val,
            step_val,
            gate_val,
            convx_val,
            convbc_val,
            bias_val,
            alog_val,
            skip_val,
            gain_val,
            mask_full,
        )

    mixed_out, pull_mixer = jax.vjp(
        local_mixer,
        inner_in,
        bc_raw,
        step_raw,
        gate,
        conv_x,
        conv_bc,
        dt_bias,
        a_log,
        dskip,
        inner_gain,
    )
    mixed_reduced = mixed_out.astype(jnp.bfloat16)
    cot_masked = (cot_half * mask_half[..., None]).astype(jnp.bfloat16)
    cotangent_whole = lax.all_gather(cot_masked, "tensor", axis=1, tiled=True)
    partial_row_block = jnp.einsum(
        "mtu,ur->mtr", mixed_reduced, output_weight, preferred_element_type=jnp.float32
    )
    mixed_half = lax.psum_scatter(partial_row_block, "tensor", scatter_dimension=1, tiled=True)
    gradient_whole = jnp.einsum(
        "mbn,pn->mbp", cotangent_whole, output_weight, preferred_element_type=jnp.float32
    )
    grad_mixed = lax.optimization_barrier(gradient_whole.astype(jnp.bfloat16)).astype(jnp.float32)
    output_local = jnp.einsum(
        "thw,thz->wz", mixed_reduced, cotangent_whole, preferred_element_type=jnp.float32
    )
    (
        grad_inner,
        grad_bc_part,
        grad_step,
        grad_gate,
        grad_convx,
        grad_convbc,
        grad_bias,
        grad_alog,
        grad_skip,
        grad_gain,
    ) = pull_mixer(grad_mixed)
    gate_low = grad_gate.astype(jnp.bfloat16)
    inner_low = grad_inner.astype(jnp.bfloat16)
    step_low = grad_step.astype(jnp.bfloat16)
    normed_part = back_project(gate_low, gate_w) + back_project(inner_low, inner_w)
    normed_part = normed_part + back_project(step_low, dt_w)
    normed_grad, bc_grad = (
        lax.psum_scatter(normed_part, "tensor", scatter_dimension=1, tiled=True),
        lax.psum_scatter(grad_bc_part, "tensor", scatter_dimension=1, tiled=True),
    )
    bc_low = bc_grad.astype(jnp.bfloat16)
    normed_grad = normed_grad + back_project(bc_low, bc_w)
    gate_wgrad = weight_grad(normed, gate_low)
    inner_wgrad = weight_grad(normed, inner_low)
    step_wgrad = weight_grad(normed, step_low)
    bc_wgrad = weight_grad(normed_half, bc_low)
    scaled_grad = normed_grad * norm_gain
    norm_part = jnp.sum(normed_grad * unit_rows, axis=(0, 1))
    rows_grad = cot_half + inv_rms * (
        scaled_grad - unit_rows * jnp.mean(scaled_grad * unit_rows, axis=-1, keepdims=True)
    )
    gate_sum, inner_sum, step_sum, out_sum = (
        lax.psum_scatter(gate_wgrad, "dp", scatter_dimension=0, tiled=True),
        lax.psum_scatter(inner_wgrad, "dp", scatter_dimension=0, tiled=True),
        lax.psum_scatter(step_wgrad, "dp", scatter_dimension=0, tiled=True),
        lax.psum_scatter(output_local, "dp", scatter_dimension=1, tiled=True),
    )
    bc_all, norm_all, convbc_all = lax.psum((bc_wgrad, norm_part, grad_convbc), ("dp", "tensor"))
    bc_rows = w_bc.shape[0]
    bc_sum = lax.dynamic_slice_in_dim(bc_all, rank_dp * bc_rows, bc_rows, 0)
    convx_sum, bias_sum, alog_sum, skip_sum, gain_sum = lax.psum(
        (grad_convx, grad_bias, grad_alog, grad_skip, grad_gain), "dp"
    )
    out_half = rows_half + mask_half[..., None] * mixed_half
    output, input_grad = (
        lax.all_to_all(
            out_half.astype(jnp.bfloat16)[:, None], "dp", split_axis=2, concat_axis=0, tiled=True
        ),
        lax.all_to_all(
            rows_grad.astype(jnp.bfloat16)[:, None], "dp", split_axis=2, concat_axis=0, tiled=True
        ),
    )
    return (
        output,
        input_grad,
        norm_all,
        gate_sum,
        inner_sum,
        bc_sum,
        step_sum,
        convx_sum,
        convbc_all,
        bias_sum,
        alog_sum,
        skip_sum,
        gain_sum,
        out_sum,
    )


def solution(mesh):
    return jax.shard_map(
        shards,
        mesh=mesh,
        in_specs=(
            P(None, "tensor", "dp", None),
            P(None, "tensor", "dp", None),
            P(),
            P(),
            P(),
            P("dp", "tensor"),
            P("dp", "tensor"),
            P("dp", None),
            P("dp", "tensor"),
            P(None, "tensor"),
            P(),
            P("tensor"),
            P("tensor"),
            P("tensor"),
            P("tensor"),
            P("tensor", "dp"),
        ),
        out_specs=(
            P(None, "tensor", "dp", None),
            P(None, "tensor", "dp", None),
            P(),
            P("dp", "tensor"),
            P("dp", "tensor"),
            P("dp", None),
            P("dp", "tensor"),
            P(None, "tensor"),
            P(),
            P("tensor"),
            P("tensor"),
            P("tensor"),
            P("tensor"),
            P("tensor", "dp"),
        ),
        check_vma=False,
    )
```

profile of v0, /device:TPU:0, one launch (start us, length us, event | category | flops | bytes accessed | tf_op | source)
XLA Modules:
  0.0 1662.7 jit_solution(1774268298412946500)
XLA Ops:
  10.7 43.2 %all_to_all.42 = bf16[16,1,64,768]{3,2,1,0:T(8,128)(2,1)S(1)} all-to-all(bf16[16,1,64,768]{3,2,1,0:T(8,128)(2,1)S(1)} %bitcast_select_fusion), channel_id=1, replica_groups=mesh['dp'=16,'tensor'=2] {'dp'}, dimensions={0} | all-to-all | bytes 3145728 | tf_op jit(solution)/shard_map/all_to_all | solution.py:130
  67.4 38.5 %all-gather = bf16[16,48,24]{1,2,0:T(8,128)(2,1)S(1)} all-gather(bf16[1,48,24]{1,2,0:T(8,128)(2,1)} %bitcast.685), channel_id=1, replica_groups=mesh['dp'=16,'tensor'=2] {'dp'}, dimensions={0}, use_global_device_ids=true | all-gather | bytes 39168 | tf_op jit(solution)/shard_map/all_gather | solution.py:150
  109.4 26.3 %all_gather.24 = bf16[768,128]{1,0:T(8,128)(2,1)} all-gather(bf16[48,128]{1,0:T(8,128)(2,1)S(1)} %copy-done.93), channel_id=1, replica_groups=mesh['dp'=16,'tensor'=2] {'dp'}, dimensions={0}, use_global_device_ids=true | all-gather | bytes 208896 | tf_op jit(solution)/shard_map/all_gather | solution.py:149
  166.0 6.5 fusion.57
  172.5 6.6 copy.612
  179.1 7.0 copy.769
  197.2 6.3 broadcast_multiply_fusion.3
  203.6 9.5 fusion.111
  216.5 34.1 %while.69 = (s32[]{:T(128)}, f32[1,12,64,64]{3,2,1,0:T(8,128)S(1)}, f32[16,1,12,64,64]{4,3,2,1,0:T(8,128)}, f32[16,1,12,1,1]{2,4,3,1,0:T(1,128)S(1)}, f32[16,1,1...) while((s32[]{:T(128)}, f32[1,12,64,64]{3,2,1,0:T(8,128)S(1)}, ...), condition=%wide.region_4.5_spmd.clone, body=%wide.region_3.4_spmd.clone.sunk | while | flops 196611 | bytes 1967868 | solution.py:46
  250.7 6.7 copy.627
  262.4 9.2 fusion.216
  276.6 6.8 broadcast_multiply_fusion.2
  283.3 12.3 rev.36
  295.7 7.0 copy.771
  306.2 9.4 fusion.114
  319.0 54.7 %while.70 = (s32[]{:T(128)}, f32[1,12,64,64]{3,2,1,0:T(8,128)S(1)}, f32[16,1,12,64,64]{4,3,2,1,0:T(8,128)}, f32[16,1,12,1,1]{2,4,3,1,0:T(1,128)S(1)}, f32[16,1,1...) while((s32[]{:T(128)}, f32[1,12,64,64]{3,2,1,0:T(8,128)S(1)}, ...), condition=%wide.region_7.8_spmd.clone, body=%wide.region_6.7_spmd.clone.sunk | while | flops 196611 | bytes 1967404 | solution.py:46
  373.7 6.7 copy.645
  380.4 9.2 fusion.218
  394.6 30.4 %bitcast_add_fusion.6 = f32[1,16,128,12,64]{2,4,3,1,0:T(8,128)} fusion(f32[16,128,12,64]{1,3,2,0:T(8,128)} %bitcast.637, f32[16,128,12]{1,2,0:T(8,128)S(1)} %copy.646, f32[16,128,12]{1,2,0:T(8,128)S(1)} %copy.636, f32[16,128,128]{2,1,0:T(8,128)} %fusion.217, pred[128,128]{1,0:T(8,128)(4,1)S(1)} %copy-done.91, f32[16,128,12,64]{1,0,3,2:T(8,128)} %bitcast.604), kind=kOutput, calls=%fused_computation.67 | convolution fusion | flops 2431647744 | bytes 20135936 | tf_op jit(solution)/shard_map/jvp(vmap(kijh,kjhp->kihp))/dot_general | solution.py:34
  424.9 29.2 %bitcast_add_fusion.7 = f32[1,16,128,12,64]{2,4,3,1,0:T(8,128)} fusion(f32[16,128,12,64]{1,3,2,0:T(8,128)S(1)} %bitcast.635, f32[16,128,12]{1,2,0:T(8,128)S(1)} %copy.628, f32[16,128,12]{1,2,0:T(8,128)S(1)} %copy.618, f32[16,128,128]{2,1,0:T(8,128)S(1)} %copy-done.46, pred[128,128]{1,0:T(8,128)(4,1)S(1)} %copy-done.91, ...), kind=kOutput, calls=%fused_computation.68 | convolution fusion | flops 2431647744 | bytes 20135936 | tf_op jit(solution)/shard_map/jvp(vmap(kijh,kjhp->kihp))/dot_general | solution.py:34
  454.8 16.1 copy.672
  472.4 9.8 copy.629
  482.1 7.1 copy.647
  495.1 12.1 rev.40
  512.4 13.8 multiply_reduce_fusion.11
  526.3 6.5 fusion.106
  546.4 12.9 fusion.144
  559.3 12.5 rev.41
  580.3 9.5 fusion.110
  593.1 51.8 %while.71 = (s32[]{:T(128)}, f32[1,12,64,64]{3,2,1,0:T(8,128)S(1)}, f32[16,1,12]{2,1,0:T(1,128)S(1)}, f32[16,1,12,64,64]{4,3,2,1,0:T(8,128)}, f32[16,1,12,64,64]...) while((s32[]{:T(128)}, f32[1,12,64,64]{3,2,1,0:T(8,128)S(1)}, ...), condition=%wide.region_13.14_spmd.clone, body=%wide.region_11.13_spmd.clone.sunk | while | flops 294904 | bytes 2164048 | solution.py:46
  645.0 15.9 fusion.37
  671.5 9.6 fusion.109
  684.6 61.6 %while.72 = (s32[]{:T(128)}, f32[1,12,64,64]{3,2,1,0:T(8,128)S(1)}, f32[16,1,12]{2,1,0:T(1,128)S(1)}, f32[16,1,12,64,64]{4,3,2,1,0:T(8,128)}, f32[16,1,12,64,64]...) while((s32[]{:T(128)}, f32[1,12,64,64]{3,2,1,0:T(8,128)S(1)}, ...), condition=%wide.region_16.17_spmd.clone, body=%wide.region_14.16_spmd.clone.sunk | while | flops 294904 | bytes 2164048 | solution.py:46
  746.3 12.4 fusion.30
  758.7 27.0 %fusion.62 = f32[16,12,128,128]{3,2,1,0:T(8,128)} fusion(f32[16,12,64,128]{3,0,2,1:T(8,128)S(1)} %bitcast.583, f32[16,128,12,64]{1,0,3,2:T(8,128)} %get-tuple-element.851), kind=kOutput, calls=%fused_computation.126 | convolution fusion | flops 2415919104 | bytes 25165824 | tf_op jit(solution)/shard_map/transpose(jvp(vmap(kijh,kjhp->kihp)))/dot_general | solution.py:34
  785.7 19.3 %fusion.36 = (f32[16,128,12]{1,2,0:T(8,128)S(1)}, f32[16,128,12]{1,2,0:T(8,128)}, f32[1,16,128,12,64]{2,4,3,1,0:T(8,128)}) fusion(f32[16,12,64,128]{3,2,1,0:T(8,128)S(1)} %fusion.30, f32[1,16,128,12,64]{2,1,0,4,3:T(8,128)S(1)} %bitcast.656, f32[16,128,12]{1,2,0:T(8,128)S(1)} %copy-done.63, f32[16,128,12]{1,2,0:T(8,128)S(1)} %copy-done.58, ...), kind=kOutput, calls=%fused_computation.79 | convolution fusion | flops 2439462912 | bytes 26722304 | tf_op jit(solution)/shard_map/transpose(jvp(vmap(kijh,kjhp->kihp)))/dot_general | solution.py:34
  807.2 13.6 fusion.130
  820.8 13.7 fusion.131
  834.6 10.6 fusion.137
  845.2 8.2 fusion.132
  853.5 10.0 copy.668
  863.5 17.6 %bitcast_add_fusion.5 = f32[1,16,128,12,64]{2,4,3,1,0:T(8,128)S(1)} fusion(f32[16,12,64,128]{3,2,1,0:T(8,128)} %get-tuple-element.904, f32[16,128,12]{1,2,0:T(8,128)S(1)} %copy-done.62, f32[16,128,12]{1,2,0:T(8,128)S(1)} %copy-done.61, f32[16,128,128]{2,1,0:T(8,128)S(1)} %copy-done.48, pred[128,128]{1,0:T(8,128)(4,1)S(1)} %copy-done.92, ...), kind=kOutput, calls=%fused_computation.66 | convolution fusion | flops 2431647744 | bytes 20135936 | tf_op jit(solution)/shard_map/transpose(jvp(vmap(kijh,kjhp->kihp)))/dot_general | solution.py:34
  891.1 12.1 rev.42
  903.2 13.4 multiply_reduce_fusion.1
  916.6 6.6 copy.670
  924.8 42.1 %fusion.19 = (f32[16,128,12]{1,2,0:T(8,128)}, f32[16,128,12]{1,2,0:T(8,128)}, f32[16,128,128]{2,1,0:T(8,128)}, f32[16,128,128]{2,1,0:T(8,128)}, f32[16,128,12]{1,2,0:T(8,128)}, /*index=5*/f32[16,128,12]{1,2,0:T(8,128)}) fusion(f32[16,128,12]{1,2,0:T(8,128)S(1)} %copy-done.61, f32[16,128,128]{2,1,0:T(8,128)} %fusion.217, ...), kind=kOutput, calls=%fused_computation.53 | convolution fusion | flops 2484502528 | bytes 29966336 | tf_op jit(solution)/shard_map/transpose(jvp(vmap(kijh,kjhp->kihp)))/dot_general | solution.py:34
  984.5 8.3 rev.43
  1049.7 14.8 multiply_reduce_fusion.4
  1087.4 7.3 convolution_bitcast_fusion
  1102.7 7.0 fusion.90
  1109.8 7.2 fusion.92
  1117.1 43.6 %reduce-scatter.12.cloned.1.call-done = f32[1,1024,768]{2,1,0:T(8,128)} async-done(((f32[1,2048,768]{2,1,0:T(8,128)}), f32[1,1024,768]{2,1,0:T(8,128)}) %reduce-scatter.12.cloned.1.call-update) | async-done | bytes 3145744 | tf_op jit(solution)/shard_map/reduce_scatter | solution.py:229
  1166.2 73.9 %reduce-scatter.10.cloned.1.call-done = f32[1,1024,768]{2,1,0:T(8,128)} async-done(((f32[1,2048,768]{2,1,0:T(8,128)}), f32[1,1024,768]{2,1,0:T(8,128)}) %reduce-scatter.10.cloned.1.call-update) | async-done | bytes 3145744 | tf_op jit(solution)/shard_map/reduce_scatter | solution.py:203
  1250.2 11.3 reduce.61
  1268.7 7.1 fusion.85
  1279.9 11.5 reduce.60
  1292.7 9.3 all-to-all-done.3
  1302.0 9.5 all-to-all-start.1
  1311.7 82.6 %all-reduce.29 = (f32[4,768]{1,0:T(4,128)}, f32[24]{0:T(128)}, f32[12]{0:T(128)}, f32[12]{0:T(128)}, f32[768]{0:T(1024)}) all-reduce(f32[4,768]{1,0:T(4,128)S(1)} %pad_add_fusion.7, f32[24]{0:T(128)S(1)} %get-tuple-element.843, f32[12]{0:T(128)S(1)} %exponential_multiply_fusion, ...), channel_id=1, replica_groups=mesh['dp'=16,'tensor'=2] {'dp'}, use_global_device_ids=true, to_apply=%region_46.47 | all-reduce | flops 3888 | bytes 31104 | tf_op jit(solution)/shard_map/psum | solution.py:252
  1395.8 59.7 %all-reduce.32.cloned.1.call-done = f32[768,128]{1,0:T(8,128)} async-done(((f32[768,128]{1,0:T(8,128)}), f32[768,128]{1,0:T(8,128)}) %all-reduce.32.cloned.1.call-update) | async-done | bytes 393232 | tf_op jit(solution)/shard_map/psum | solution.py:249
  1456.9 39.4 %all-reduce.28 = (f32[768]{0:T(1024)}, f32[4,128]{1,0:T(4,128)}) all-reduce(f32[768]{0:T(1024)S(1)} %get-tuple-element.766, f32[4,128]{1,0:T(4,128)S(1)} %pad_add_fusion.8), channel_id=1, replica_groups=mesh['dp'=16,'tensor'=2] {'dp','tensor'}, use_global_device_ids=true, to_apply=%region_37.38 | all-reduce | flops 1280 | bytes 10240 | tf_op jit(solution)/shard_map/psum | solution.py:249
  1505.9 10.0 reshape.1526
  1523.0 66.2 %reduce-scatter.16.cloned.1.call-done = f32[48,768]{1,0:T(8,128)} async-done(((f32[768,768]{1,0:T(8,128)}), f32[48,768]{1,0:T(8,128)}) %reduce-scatter.16.cloned.1.call-update) | async-done | bytes 147472 | tf_op jit(solution)/shard_map/reduce_scatter | solution.py:244
  1589.2 66.8 %reduce-scatter.20.cloned.1.call-done = f32[768,48]{0,1:T(8,128)} async-done(((f32[768,768]{0,1:T(8,128)}), f32[768,48]{0,1:T(8,128)}) %reduce-scatter.20.cloned.1.call-update) | async-done | bytes 147472 | tf_op jit(solution)/shard_map/reduce_scatter | solution.py:247
  (825 shorter events, 503.7 us)
Async XLA Ops:
  7.2 47.2 %copy-start.74 = (f32[768]{0:T(1024)S(1)}, f32[768]{0:T(1024)}, u32[]{:S(2)}) copy-start(f32[768]{0:T(1024)} %param.28) | copy-start | bytes 9220
  7.2 134.2 %all-gather.7.cloned.1.call-start = ((), (), s32[]{:S(2)}) async-start(), calls=%async_computation.11 | async-start | bytes 4718592 | tf_op jit(solution)/shard_map/all_gather | solution.py:145
  53.9 52.9 %copy-start.103 = (f32[768]{0:T(1024)S(1)}, f32[768]{0:T(1024)}, u32[]{:S(2)}) copy-start(f32[768]{0:T(1024)} %param.38) | copy-start | bytes 9220
  53.9 55.5 %copy-start.93 = (bf16[48,128]{1,0:T(8,128)(2,1)S(1)}, bf16[48,128]{1,0:T(8,128)(2,1)}, u32[]{:S(2)}) copy-start(bf16[48,128]{1,0:T(8,128)(2,1)} %param.31) | copy-start | bytes 36868
  57.0 103.9 %all-gather.9.cloned.1.call-start = ((), (), s32[]{:S(2)}) async-start(), calls=%async_computation.12 | async-start | bytes 1253376 | tf_op jit(solution)/shard_map/all_gather | solution.py:148
  57.8 449.5 %all-gather.11.cloned.1.call-start = ((), (), s32[]{:S(2)}) async-start(), calls=%async_computation.13 | async-start | bytes 1253376 | tf_op jit(solution)/shard_map/all_gather | solution.py:147
  58.5 80.7 %all-to-all-start.2 = ((bf16[16,1,64,768]{3,2,1,0:T(8,128)(2,1)}), bf16[16,1,64,768]{3,2,1,0:T(8,128)(2,1)S(1)}, u32[]{:S(2)}, u32[]{:S(2)}) async-start(bf16[16,1,64,768]{3,2,1,0:T(8,128)(2,1)} %param.25), calls=%async_computation.3 | async-start | bytes 3145728 | tf_op jit(solution)/shard_map/all_to_all | solution.py:131
  63.5 462.7 %all-gather.13.cloned.1.call-start = ((), (), s32[]{:S(2)}) async-start(), calls=%async_computation.14 | async-start | bytes 1253376 | tf_op jit(solution)/shard_map/all_gather | solution.py:151
  64.1 462.1 %all-gather.15.cloned.1.call-start = ((), (), s32[]{:S(2)}) async-start(), calls=%async_computation.16 | async-start | bytes 4718592 | tf_op jit(solution)/shard_map/all_gather | solution.py:199
  106.1 38.8 %copy-start.55 = (bf16[768,24]{0,1:T(8,128)(2,1)}, bf16[768,24]{0,1:T(8,128)(2,1)S(1)}, u32[]{:S(2)}) copy-start(bf16[768,24]{0,1:T(8,128)(2,1)S(1)} %reshape.1504) | copy-start | bytes 110596
  106.8 39.1 %copy-start.105 = (f32[12]{0:T(128)}, f32[12]{0:T(128)S(1)}, u32[]{:S(2)}) copy-start(f32[12]{0:T(128)S(1)} %exp.196) | copy-start | bytes 148
  135.7 25.1 %copy-start.65 = (f32[2048]{0:T(1024)}, f32[2048]{0:T(1024)S(1)}, u32[]{:S(2)}) copy-start(f32[2048]{0:T(1024)S(1)} %fusion.193) | copy-start | bytes 24580
  140.9 959.4 %reduce-scatter.14.cloned.1.call-start = ((), (), s32[]{:S(2)}) async-start(), calls=%async_computation.18 | async-start | bytes 1572864 | tf_op jit(solution)/shard_map/reduce_scatter | solution.py:230
  149.5 16.4 copy-start.27
  149.5 36.5 %copy-start.67 = (f32[16,12]{1,0:T(8,128)}, f32[16,12]{1,0:T(8,128)S(1)}, u32[]{:S(2)}) copy-start(f32[16,12]{1,0:T(8,128)S(1)} %get-tuple-element.876) | copy-start | bytes 2308
  159.7 143.0 %copy-start.69 = (f32[16,12]{1,0:T(8,128)}, f32[16,12]{1,0:T(8,128)S(1)}, u32[]{:S(2)}) copy-start(f32[16,12]{1,0:T(8,128)S(1)} %get-tuple-element.878) | copy-start | bytes 2308
  160.8 115.7 %copy-start.42 = (f32[2048,12]{0,1:T(8,128)}, f32[2048,12]{0,1:T(8,128)S(1)}, u32[]{:S(2)}) copy-start(f32[2048,12]{0,1:T(8,128)S(1)} %get-tuple-element.883) | copy-start | bytes 294916
  192.0 79.6 %copy-start.9 = (f32[1,2048,64]{2,1,0:T(8,128)}, f32[1,2048,64]{2,1,0:T(8,128)S(1)}, u32[]{:S(2)}) copy-start(f32[1,2048,64]{2,1,0:T(8,128)S(1)} %get-tuple-element.880) | copy-start | bytes 1572868
  276.6 148.4 %copy-start.57 = (f32[16,128,12]{1,2,0:T(8,128)}, f32[16,128,12]{1,2,0:T(8,128)S(1)}, u32[]{:S(2)}) copy-start(f32[16,128,12]{1,2,0:T(8,128)S(1)} %copy.618) | copy-start | bytes 294916
  392.8 187.4 %copy-start.40 = (f32[16,128,12]{1,2,0:T(8,128)}, f32[16,128,12]{1,2,0:T(8,128)S(1)}, u32[]{:S(2)}) copy-start(f32[16,128,12]{1,2,0:T(8,128)S(1)} %copy.646) | copy-start | bytes 294916
  394.5 30.4 %copy-start.60 = (f32[16,128,12]{1,2,0:T(8,128)}, f32[16,128,12]{1,2,0:T(8,128)S(1)}, u32[]{:S(2)}) copy-start(f32[16,128,12]{1,2,0:T(8,128)S(1)} %copy.636) | copy-start | bytes 294916
  394.5 30.4 %copy-start.22 = (f32[16,128,768]{1,2,0:S(1)}, f32[16,128,768]{1,2,0}, u32[]{:S(2)}) copy-start(f32[16,128,768]{1,2,0} %fusion.216) | copy-start | bytes 18874372
  394.5 30.4 %copy-start.46 = (f32[16,128,128]{2,1,0:T(8,128)S(1)}, f32[16,128,128]{2,1,0:T(8,128)}, u32[]{:S(2)}) copy-start(f32[16,128,128]{2,1,0:T(8,128)} %fusion.215) | copy-start | bytes 3145732
  645.0 15.9 copy-start.89
  684.6 61.6 %copy-start.10 = (f32[1,2048,64]{2,1,0:T(8,128)S(1)}, f32[1,2048,64]{2,1,0:T(8,128)}, u32[]{:S(2)}) copy-start(f32[1,2048,64]{2,1,0:T(8,128)} %copy-done.9) | copy-start | bytes 1572868
  746.2 39.5 %slice-start.6 = ((s8[6291456]{0:T(1024)(128)(4,1)}), s8[4194304]{0:T(1024)(128)(4,1)S(1)}, s32[]{:S(2)}) async-start(s8[6291456]{0:T(1024)(128)(4,1)} %bitcast.654), calls=%async_computation.30 | async-start | bytes 8388608
  758.7 27.0 %slice-start.7 = ((s8[6291456]{0:T(1024)(128)(4,1)}), s8[2097152]{0:T(1024)(128)(4,1)S(1)}, s32[]{:S(2)}) async-start(s8[6291456]{0:T(1024)(128)(4,1)} %bitcast.654), calls=%async_computation.31 | async-start | bytes 4194304
  758.7 27.0 %copy-start.47 = (f32[16,128,128]{2,1,0:T(8,128)S(1)}, f32[16,128,128]{2,1,0:T(8,128)}, u32[]{:S(2)}) copy-start(f32[16,128,128]{2,1,0:T(8,128)} %fusion.215) | copy-start | bytes 3145732
  758.7 27.0 %copy-start.58 = (f32[16,128,12]{1,2,0:T(8,128)S(1)}, f32[16,128,12]{1,2,0:T(8,128)}, u32[]{:S(2)}) copy-start(f32[16,128,12]{1,2,0:T(8,128)} %copy-done.57) | copy-start | bytes 294916
  758.7 27.0 %copy-start.63 = (f32[16,128,12]{1,2,0:T(8,128)S(1)}, f32[16,128,12]{1,2,0:T(8,128)}, u32[]{:S(2)}) copy-start(f32[16,128,12]{1,2,0:T(8,128)} %copy.691) | copy-start | bytes 294916
  758.7 27.0 %copy-start.64 = (f32[16,128,12]{1,2,0:T(8,128)S(1)}, f32[16,128,12]{1,2,0:T(8,128)}, u32[]{:S(2)}) copy-start(f32[16,128,12]{1,2,0:T(8,128)} %copy.666) | copy-start | bytes 294916
  807.2 37.9 %slice-start.2 = ((s8[6291456]{0:T(1024)(128)(4,1)}), s8[4194304]{0:T(1024)(128)(4,1)S(1)}, s32[]{:S(2)}) async-start(s8[6291456]{0:T(1024)(128)(4,1)} %bitcast.599), calls=%async_computation.26 | async-start | bytes 8388608
  807.2 37.9 %slice-start.4 = ((s8[6291456]{0:T(1024)(128)(4,1)}), s8[4194304]{0:T(1024)(128)(4,1)S(1)}, s32[]{:S(2)}) async-start(s8[6291456]{0:T(1024)(128)(4,1)} %bitcast.607), calls=%async_computation.28 | async-start | bytes 8388608
  820.8 24.3 %slice-start.3 = ((s8[6291456]{0:T(1024)(128)(4,1)}), s8[2097152]{0:T(1024)(128)(4,1)S(1)}, s32[]{:S(2)}) async-start(s8[6291456]{0:T(1024)(128)(4,1)} %bitcast.599), calls=%async_computation.27 | async-start | bytes 4194304
  820.8 24.3 %slice-start.5 = ((s8[6291456]{0:T(1024)(128)(4,1)}), s8[2097152]{0:T(1024)(128)(4,1)S(1)}, s32[]{:S(2)}) async-start(s8[6291456]{0:T(1024)(128)(4,1)} %bitcast.607), calls=%async_computation.29 | async-start | bytes 4194304
  834.6 28.9 %slice-start = ((s8[6291456]{0:T(1024)(128)(4,1)}), s8[4194304]{0:T(1024)(128)(4,1)S(1)}, s32[]{:S(2)}) async-start(s8[6291456]{0:T(1024)(128)(4,1)} %bitcast.595), calls=%async_computation.24 | async-start | bytes 8388608
  845.2 18.3 %slice-start.1 = ((s8[6291456]{0:T(1024)(128)(4,1)}), s8[2097152]{0:T(1024)(128)(4,1)S(1)}, s32[]{:S(2)}) async-start(s8[6291456]{0:T(1024)(128)(4,1)} %bitcast.595), calls=%async_computation.25 | async-start | bytes 4194304
  924.8 46.8 %copy-start.51 = (f32[16,128,12]{1,2,0:T(8,128)S(1)}, f32[16,128,12]{1,2,0:T(8,128)}, u32[]{:S(2)}) copy-start(f32[16,128,12]{1,2,0:T(8,128)} %multiply_reduce_fusion.7) | copy-start | bytes 294916
  924.8 49.7 %copy-start.70 = (f32[16,12]{1,0:T(8,128)S(1)}, f32[16,12]{1,0:T(8,128)}, u32[]{:S(2)}) copy-start(f32[16,12]{1,0:T(8,128)} %copy-done.69) | copy-start | bytes 2308
  969.3 28.3 %copy-start.52 = (f32[16,128,12]{1,2,0:T(8,128)S(1)}, f32[16,128,12]{1,2,0:T(8,128)}, u32[]{:S(2)}) copy-start(f32[16,128,12]{1,2,0:T(8,128)} %multiply_reduce_fusion.6) | copy-start | bytes 294916
  971.6 27.3 %copy-start.90 = (f32[16,12]{0,1:T(8,128)S(1)}, f32[16,12]{0,1:T(8,128)}, u32[]{:S(2)}) copy-start(f32[16,12]{0,1:T(8,128)} %fusion.189) | copy-start | bytes 2308
  971.6 28.1 %copy-start.68 = (f32[16,12]{1,0:T(8,128)S(1)}, f32[16,12]{1,0:T(8,128)}, u32[]{:S(2)}) copy-start(f32[16,12]{1,0:T(8,128)} %copy-done.67) | copy-start | bytes 2308
  980.6 28.4 %copy-start.66 = (f32[2048]{0:T(1024)S(1)}, f32[2048]{0:T(1024)}, u32[]{:S(2)}) copy-start(f32[2048]{0:T(1024)} %copy-done.65) | copy-start | bytes 24580
  982.9 27.1 %copy-start.38 = (f32[1,2048,12,2]{1,3,2,0:T(2,128)S(1)}, f32[1,2048,12,2]{1,3,2,0:T(2,128)}, u32[]{:S(2)}) copy-start(f32[1,2048,12,2]{1,3,2,0:T(2,128)} %copy-done.37) | copy-start | bytes 589828
  982.9 27.1 %copy-start.106 = (f32[12]{0:T(128)S(1)}, f32[12]{0:T(128)}, u32[]{:S(2)}) copy-start(f32[12]{0:T(128)} %copy-done.105) | copy-start | bytes 148
  1049.6 111.1 %reduce-scatter.12.cloned.1.call-start = ((), (), s32[]{:S(2)}) async-start(), calls=%async_computation.17 | async-start | bytes 9437184 | tf_op jit(solution)/shard_map/reduce_scatter | solution.py:229
  1049.6 14.8 copy-start.81
  1086.1 153.9 %reduce-scatter.10.cloned.1.call-start = ((), (), s32[]{:S(2)}) async-start(), calls=%async_computation.15 | async-start | bytes 9437184 | tf_op jit(solution)/shard_map/reduce_scatter | solution.py:203
  1094.7 299.7 %reduce-scatter.22.cloned.1.call-start = ((), (), s32[]{:S(2)}) async-start(), calls=%async_computation.23 | async-start | bytes 417792
  1100.2 355.3 %all-reduce.32.cloned.1.call-start = ((), (), s32[]{:S(2)}) async-start(), calls=%async_computation.21 | async-start | bytes 786432 | tf_op jit(solution)/shard_map/psum | solution.py:249
  1102.7 420.3 %reduce-scatter.18.cloned.1.call-start = ((), (), s32[]{:S(2)}) async-start(), calls=%async_computation.20 | async-start | bytes 2506752 | tf_op jit(solution)/shard_map/reduce_scatter | solution.py:245
  1109.7 50.9 %copy-start.34 = (f32[1,1024,128]{2,1,0:T(8,128)S(1)}, f32[1,1024,128]{2,1,0:T(8,128)}, u32[]{:S(2)}) copy-start(f32[1,1024,128]{2,1,0:T(8,128)} %reduce-scatter.14.cloned.1.call-done) | copy-start | bytes 1572868
  1109.7 50.9 %copy-start.36 = (bf16[768,128]{1,0:T(8,128)(2,1)S(1)}, bf16[768,128]{1,0:T(8,128)(2,1)}, u32[]{:S(2)}) copy-start(bf16[768,128]{1,0:T(8,128)(2,1)} %all_gather.24) | copy-start | bytes 589828
  1109.7 50.9 %copy-start.77 = (f32[1024]{0:T(1024)S(1)}, f32[1024]{0:T(1024)}, u32[]{:S(2)}) copy-start(f32[1024]{0:T(1024)} %copy-done.76) | copy-start | bytes 12292
  1109.7 479.4 %reduce-scatter.16.cloned.1.call-start = ((), (), s32[]{:S(2)}) async-start(), calls=%async_computation.19 | async-start | bytes 2506752 | tf_op jit(solution)/shard_map/reduce_scatter | solution.py:244
  1117.0 123.0 %copy-start.30 = (bf16[16,1,64,768]{3,2,1,0:T(8,128)(2,1)S(1)}, bf16[16,1,64,768]{3,2,1,0:T(8,128)(2,1)}, u32[]{:S(2)}) copy-start(bf16[16,1,64,768]{3,2,1,0:T(8,128)(2,1)} %copy-done.29) | copy-start | bytes 4718596
  1117.0 123.0 %copy-start.79 = (f32[1,1024]{1,0:T(1,128)S(1)}, f32[1,1024]{1,0:T(1,128)}, u32[]{:S(2)}) copy-start(f32[1,1024]{1,0:T(1,128)} %copy-done.78) | copy-start | bytes 12292
  1262.9 39.1 %all-to-all-start.3 = ((bf16[16,2,24576]{2,1,0:T(2,128)(2,1)}), bf16[16,2,24576]{2,1,0:T(2,128)(2,1)S(1)}, u32[]{:S(2)}, u32[]{:S(2)}) async-start(bf16[16,2,24576]{2,1,0:T(2,128)(2,1)} %reshape.1527), calls=%async_computation.6 | async-start | bytes 3145728 | tf_op jit(solution)/shard_map/all_to_all | solution.py:260
  1268.5 387.5 %reduce-scatter.20.cloned.1.call-start = ((), (), s32[]{:S(2)}) async-start(), calls=%async_computation.22 | async-start | bytes 2506752 | tf_op jit(solution)/shard_map/reduce_scatter | solution.py:247
  1279.9 31.6 %copy-start.88 = (f32[12,64]{1,0:T(8,128)S(1)}, f32[12,64]{1,0:T(8,128)}, u32[]{:S(2)}) copy-start(f32[12,64]{1,0:T(8,128)} %get-tuple-element.761) | copy-start | bytes 9220
  1279.9 31.7 %copy-start.111 = (f32[12]{0:T(128)S(1)}, f32[12]{0:T(128)}, u32[]{:S(2)}) copy-start(f32[12]{0:T(128)} %param.36) | copy-start | bytes 148
  1279.9 31.8 %copy-start.107 = (f32[12]{0:T(128)S(1)}, f32[12]{0:T(128)}, u32[]{:S(2)}) copy-start(f32[12]{0:T(128)} %get-tuple-element.768) | copy-start | bytes 148
  1302.0 203.9 %all-to-all-start.1 = ((bf16[16,2,24576]{2,1,0:T(2,128)(2,1)}), bf16[16,2,24576]{2,1,0:T(2,128)(2,1)}, u32[]{:S(2)}, u32[]{:S(2)}) async-start(bf16[16,2,24576]{2,1,0:T(2,128)(2,1)} %reshape.1525), calls=%async_computation.2 | async-start | bytes 3145728 | tf_op jit(solution)/shard_map/all_to_all | solution.py:257
  1502.5 153.5 %copy-start.1 = (bf16[16,1,64,768]{3,2,1,0:T(8,128)(2,1)S(1)}, bf16[16,1,64,768]{3,2,1,0:T(8,128)(2,1)}, u32[]{:S(2)}) copy-start(bf16[16,1,64,768]{3,2,1,0:T(8,128)(2,1)} %param.24) | copy-start | bytes 4718596
  (73 other events, 480.3 us)
Sparse Core Ops, SparseCore 0:
  57.1 45.2 all-gather.6
  104.7 38.4 all-gather.8
  145.5 37.3 all-gather.10
  185.0 37.2 all-gather.12
  224.3 43.8 all-gather.14
  1049.7 17.6 reduce-scatter.13
  1086.3 74.3 reduce-scatter.11
  1163.0 77.0 reduce-scatter.9
  1243.9 71.1 reduce-scatter.21
  1320.3 135.1 all-reduce.31
  1460.3 62.5 reduce-scatter.17
  1527.2 61.9 reduce-scatter.15
  1594.0 61.9 reduce-scatter.19
where the time goes:
time: 1680 us; the launch traced here: 1660 us
  local copies, waits for them, and re-layouts  414 us (25%)
  matrix products  390 us (23%)
  waiting for transfers between devices  325 us (19%)
  other arithmetic  260 us (15%)
  blocking collectives  230 us (14%)
  starting transfers between devices  21.6 us (1%)
  between operations  18.3 us (1%)
    dot_general x6, matrix products, strict_scan(): jnp.einsum('kijh,kjhp->kihp', weights_in, blocked, precision=exact_prec)  165 us
    psum x1, blocking collectives, shards(): lax.psum((grad_convx, grad_bias, grad_alog, grad_skip, grad_gain), 'dp')  82.6 us
    dynamic_slice x128, local copies, waits for them, and re-layouts, strict_scan(): _, entering = lax.scan(carry_step, start_state, (block_decay, block_states))  75.8 us
    reduce_scatter x1, waiting for transfers between devices, shards(): lax.psum_scatter(partial_row_block, 'tensor', scatter_dimension=1, tiled=...  73.9 us
    reduce_scatter x1, waiting for transfers between devices, shards(): lax.psum_scatter(output_local, 'dp', scatter_dimension=1, tiled=True)  66.8 us
    reduce_scatter x1, waiting for transfers between devices, shards(): lax.psum_scatter(gate_wgrad, 'dp', scatter_dimension=0, tiled=True)  66.2 us
    dot_general x6, matrix products, strict_scan(): jnp.einsum('kjn,kjhp->khnp', in_maps, blocked * to_end[..., None], precis...  66 us
    psum x1, waiting for transfers between devices, shards(): lax.psum((bc_wgrad, norm_part, grad_convbc), ('dp', 'tensor'))  59.7 us
  transfers between devices with their start and end apart: 16, of which 7 were waited for; matrix products, arithmetic and copies ran while one was open for 32% of the time, Pallas kernels for 0%

commit v1 on v0

--- a/solution.py
+++ b/solution.py
@@ -5,6 +5,14 @@
 
 BLOCK = 128
 exact_prec = lax.Precision.HIGHEST
+
+
+def make_knots_now(matrix):
+    along_axis = "tensor"
+    mesh_dim = "dp"
+    for rr in (along_axis, mesh_dim):
+        matrix = lax.psum(matrix, rr)
+    return matrix
 
 
 def causal_conv(values, kernel):
@@ -246,7 +254,7 @@
         lax.psum_scatter(step_wgrad, "dp", scatter_dimension=0, tiled=True),
         lax.psum_scatter(output_local, "dp", scatter_dimension=1, tiled=True),
     )
-    bc_all, norm_all, convbc_all = lax.psum((bc_wgrad, norm_part, grad_convbc), ("dp", "tensor"))
+    bc_all, norm_all, convbc_all = make_knots_now((bc_wgrad, norm_part, grad_convbc))
     bc_rows = w_bc.shape[0]
     bc_sum = lax.dynamic_slice_in_dim(bc_all, rank_dp * bc_rows, bc_rows, 0)
     convx_sum, bias_sum, alog_sum, skip_sum, gain_sum = lax.psum(

time: 1680 us -> 1680 us (level)
  blocking collectives: 230 us -> 172 us
  waiting for transfers between devices: 325 us -> 366 us
  other arithmetic: 260 us -> 287 us
    psum x2, blocking collectives: 122 us -> 63.1 us  [make_knots_now(): matrix = lax.psum(matrix, rr)]
    psum x1 -> x2, waiting for transfers between devices: 59.7 us -> 105 us  [make_knots_now(): matrix = lax.psum(matrix, rr)]
    reduce_scatter x1, waiting for transfers between devices: 43.6 us -> 64.2 us  [shards(): lax.psum_scatter(normed_part, 'tensor', scatter_dimension=1, tiled=True)]
    reduce_scatter x1, waiting for transfers between devices: 66.2 us -> 45.7 us  [shards(): lax.psum_scatter(gate_wgrad, 'dp', scatter_dimension=0, tiled=True)]
    another operation x4, other arithmetic: 14.9 us -> 32.3 us  [strict_scan(): jnp.cumsum(log_decay.reshape(blocks, BLOCK, head_count), axis=1)]
    unnamed x258 -> x306, local copies, waits for them, and re-layouts: 56.8 us -> 55.4 us
  transfers between devices with their start and end apart: 16 -> 17, of which waited for: 7 -> 7; matrix products, arithmetic and copies ran while one was open for 32% -> 36% of each run, Pallas kernels for 0% -> 0%
where the time goes in v1:
time: 1680 us; the launch traced here: 1670 us
  local copies, waits for them, and re-layouts  403 us (24%)
  matrix products  401 us (24%)
  waiting for transfers between devices  366 us (22%)
  other arithmetic  287 us (17%)
  blocking collectives  172 us (10%)
  starting transfers between devices  21.3 us (1%)
  between operations  18.8 us (1%)
    dot_general x6, matrix products, strict_scan(): jnp.einsum('kijh,kjhp->kihp', weights_in, blocked, precision=exact_prec)  166 us
    psum x2, waiting for transfers between devices, make_knots_now(): matrix = lax.psum(matrix, rr)  105 us
    dynamic_slice x128, local copies, waits for them, and re-layouts, strict_scan(): _, entering = lax.scan(carry_step, start_state, (block_decay, block_states))  75.8 us
    reduce_scatter x1, waiting for transfers between devices, shards(): lax.psum_scatter(partial_row_block, 'tensor', scatter_dimension=1, tiled=...  73.9 us
    dot_general x6, matrix products, strict_scan(): jnp.einsum('kjn,kjhp->khnp', in_maps, blocked * to_end[..., None], precis...  72 us
    reduce_scatter x1, waiting for transfers between devices, shards(): lax.psum_scatter(output_local, 'dp', scatter_dimension=1, tiled=True)  66.3 us
    reduce_scatter x1, waiting for transfers between devices, shards(): lax.psum_scatter(normed_part, 'tensor', scatter_dimension=1, tiled=True)  64.2 us
    psum x2, blocking collectives, make_knots_now(): matrix = lax.psum(matrix, rr)  63.1 us
  transfers between devices with their start and end apart: 17, of which 7 were waited for; matrix products, arithmetic and copies ran while one was open for 36% of the time, Pallas kernels for 0%

profile of v1, /device:TPU:0, one launch (start us, length us, event | category | flops | bytes accessed | tf_op | source)
XLA Modules:
  0.0 1671.6 jit_solution(4122595757990117091)
XLA Ops:
  10.2 43.2 %all_to_all.42 = bf16[16,1,64,768]{3,2,1,0:T(8,128)(2,1)S(1)} all-to-all(bf16[16,1,64,768]{3,2,1,0:T(8,128)(2,1)S(1)} %bitcast_select_fusion), channel_id=1, replica_groups=mesh['dp'=16,'tensor'=2] {'dp'}, dimensions={0} | all-to-all | bytes 3145728 | tf_op jit(solution)/shard_map/all_to_all | solution.py:138
  66.4 39.1 %all-gather = bf16[16,48,24]{1,2,0:T(8,128)(2,1)S(1)} all-gather(bf16[1,48,24]{1,2,0:T(8,128)(2,1)S(1)} %bitcast.683), channel_id=1, replica_groups=mesh['dp'=16,'tensor'=2] {'dp'}, dimensions={0}, use_global_device_ids=true | all-gather | bytes 39168 | tf_op jit(solution)/shard_map/all_gather | solution.py:158
  107.6 26.2 %all_gather.24 = bf16[768,128]{1,0:T(8,128)(2,1)} all-gather(bf16[48,128]{1,0:T(8,128)(2,1)S(1)} %copy-done.112), channel_id=1, replica_groups=mesh['dp'=16,'tensor'=2] {'dp'}, dimensions={0}, use_global_device_ids=true | all-gather | bytes 208896 | tf_op jit(solution)/shard_map/all_gather | solution.py:157
  145.1 23.8 %fusion.213 = f32[1,16,128,12]{3,1,2,0:T(8,128)S(1)} fusion(f32[1,16,128,12]{3,1,2,0:T(8,128)S(1)} %copy.616), kind=kOutput, calls=%fused_computation.343 | output fusion | flops 3121152 | bytes 196608 | tf_op jit(solution)/shard_map/jvp(vmap(jit(cumsum)))/reduce_window_sum | solution.py:34
  181.7 6.8 fusion.57
  195.0 6.9 copy.769
  220.0 9.5 fusion.111
  233.0 54.6 %while.69 = (s32[]{:T(128)}, f32[1,12,64,64]{3,2,1,0:T(8,128)S(1)}, f32[16,1,12,64,64]{4,3,2,1,0:T(8,128)}, f32[16,1,12,1,1]{2,4,3,1,0:T(1,128)S(1)}, f32[16,1,1...) while((s32[]{:T(128)}, f32[1,12,64,64]{3,2,1,0:T(8,128)S(1)}, ...), condition=%wide.region_4.5_spmd.clone, body=%wide.region_3.4_spmd.clone.sunk | while | flops 196611 | bytes 1967404 | solution.py:54
  287.6 6.6 copy.627
  299.4 9.2 fusion.216
  314.8 6.6 broadcast_multiply_fusion.2
  321.4 12.3 rev.36
  333.7 6.9 copy.771
  344.6 9.5 fusion.114
  357.6 54.7 %while.70 = (s32[]{:T(128)}, f32[1,12,64,64]{3,2,1,0:T(8,128)S(1)}, f32[16,1,12,64,64]{4,3,2,1,0:T(8,128)}, f32[16,1,12,1,1]{2,4,3,1,0:T(1,128)S(1)}, f32[16,1,1...) while((s32[]{:T(128)}, f32[1,12,64,64]{3,2,1,0:T(8,128)S(1)}, ...), condition=%wide.region_7.8_spmd.clone, body=%wide.region_6.7_spmd.clone.sunk | while | flops 196611 | bytes 1967404 | solution.py:54
  412.3 6.6 copy.645
  418.9 9.9 fusion.218
  433.9 29.8 %bitcast_add_fusion.6 = f32[1,16,128,12,64]{2,4,3,1,0:T(8,128)} fusion(f32[16,128,12,64]{1,3,2,0:T(8,128)} %bitcast.635, f32[16,128,12]{1,2,0:T(8,128)S(1)} %copy.646, f32[16,128,12]{1,2,0:T(8,128)S(1)} %copy.636, f32[16,128,128]{2,1,0:T(8,128)} %fusion.217, pred[128,128]{1,0:T(8,128)(4,1)S(1)} %copy-done.110, f32[16,128,12,64]{1,0,3,2:T(8,128)} %bitcast.604), kind=kOutput, calls=%fused_computation.67 | convolution fusion | flops 2431647744 | bytes 20135936 | tf_op jit(solution)/shard_map/jvp(vmap(kijh,kjhp->kihp))/dot_general | solution.py:42
  463.7 29.2 %bitcast_add_fusion.7 = f32[1,16,128,12,64]{2,4,3,1,0:T(8,128)} fusion(f32[16,128,12,64]{1,3,2,0:T(8,128)S(1)} %bitcast.634, f32[16,128,12]{1,2,0:T(8,128)S(1)} %copy-done.53, f32[16,128,12]{1,2,0:T(8,128)S(1)} %copy-done.73, f32[16,128,128]{2,1,0:T(8,128)S(1)} %copy-done.60, pred[128,128]{1,0:T(8,128)(4,1)S(1)} %copy-done.110, ...), kind=kOutput, calls=%fused_computation.68 | convolution fusion | flops 2431647744 | bytes 20135936 | tf_op jit(solution)/shard_map/jvp(vmap(kijh,kjhp->kihp))/dot_general | solution.py:42
  493.6 16.1 copy.672
  511.1 9.7 copy.629
  520.8 7.1 copy.647
  534.1 12.2 rev.40
  551.5 13.7 multiply_reduce_fusion.11
  585.4 12.9 fusion.144
  598.3 12.2 rev.41
  614.8 13.5 fusion.130
  628.3 9.4 fusion.109
  641.1 51.8 %while.72 = (s32[]{:T(128)}, f32[1,12,64,64]{3,2,1,0:T(8,128)S(1)}, f32[16,1,12]{2,1,0:T(1,128)S(1)}, f32[16,1,12,64,64]{4,3,2,1,0:T(8,128)}, f32[16,1,12,64,64]...) while((s32[]{:T(128)}, f32[1,12,64,64]{3,2,1,0:T(8,128)S(1)}, ...), condition=%wide.region_16.17_spmd.clone, body=%wide.region_14.16_spmd.clone.sunk | while | flops 294904 | bytes 2164048 | solution.py:54
  693.0 13.4 fusion.30
  706.4 10.3 fusion.137
  721.1 9.0 fusion.131
  734.1 9.5 fusion.110
  747.1 51.8 %while.71 = (s32[]{:T(128)}, f32[1,12,64,64]{3,2,1,0:T(8,128)S(1)}, f32[16,1,12]{2,1,0:T(1,128)S(1)}, f32[16,1,12,64,64]{4,3,2,1,0:T(8,128)}, f32[16,1,12,64,64]...) while((s32[]{:T(128)}, f32[1,12,64,64]{3,2,1,0:T(8,128)S(1)}, ...), condition=%wide.region_13.14_spmd.clone, body=%wide.region_11.13_spmd.clone.sunk | while | flops 294904 | bytes 2164048 | solution.py:54
  798.9 13.7 fusion.132
  812.6 15.6 fusion.37
  829.8 7.2 multiply_reduce_fusion.6
  837.1 27.1 %fusion.62 = f32[16,12,128,128]{3,2,1,0:T(8,128)} fusion(f32[16,12,64,128]{3,0,2,1:T(8,128)} %bitcast.583, f32[16,128,12,64]{1,0,3,2:T(8,128)} %get-tuple-element.853), kind=kOutput, calls=%fused_computation.126 | convolution fusion | flops 2415919104 | bytes 25165824 | tf_op jit(solution)/shard_map/transpose(jvp(vmap(kijh,kjhp->kihp)))/dot_general | solution.py:42
  864.3 20.3 %fusion.36 = (f32[16,128,12]{1,2,0:T(8,128)S(1)}, f32[16,128,12]{1,2,0:T(8,128)}, f32[1,16,128,12,64]{2,4,3,1,0:T(8,128)}) fusion(f32[16,12,64,128]{3,2,1,0:T(8,128)S(1)} %bitcast.655, f32[1,16,128,12,64]{2,1,0,4,3:T(8,128)S(1)} %bitcast.652, f32[16,128,12]{1,2,0:T(8,128)S(1)} %copy-done.82, f32[16,128,12]{1,2,0:T(8,128)S(1)} %copy-done.74, ...), kind=kOutput, calls=%fused_computation.79 | convolution fusion | flops 2439462912 | bytes 26722304 | tf_op jit(solution)/shard_map/transpose(jvp(vmap(kijh,kjhp->kihp)))/dot_general | solution.py:42
  886.8 10.0 copy.668
  896.7 18.0 %bitcast_add_fusion.5 = f32[1,16,128,12,64]{2,4,3,1,0:T(8,128)S(1)} fusion(f32[16,12,64,128]{3,2,1,0:T(8,128)} %get-tuple-element.906, f32[16,128,12]{1,2,0:T(8,128)S(1)} %copy-done.81, f32[16,128,12]{1,2,0:T(8,128)S(1)} %copy-done.76, f32[16,128,128]{2,1,0:T(8,128)S(1)} %copy-done.62, pred[128,128]{1,0:T(8,128)(4,1)S(1)} %copy-done.110, ...), kind=kOutput, calls=%fused_computation.66 | convolution fusion | flops 2431647744 | bytes 20135936 | tf_op jit(solution)/shard_map/transpose(jvp(vmap(kijh,kjhp->kihp)))/dot_general | solution.py:42
  924.8 12.1 rev.42
  936.9 13.3 multiply_reduce_fusion.1
  956.8 41.9 %fusion.19 = (f32[16,128,12]{1,2,0:T(8,128)}, f32[16,128,12]{1,2,0:T(8,128)}, f32[16,128,128]{2,1,0:T(8,128)}, f32[16,128,128]{2,1,0:T(8,128)S(1)}, f32[16,128,12]{1,2,0:T(8,128)}, /*index=5*/f32[16,128,12]{1,2,0:T(8,128)}) fusion(f32[16,128,12]{1,2,0:T(8,128)S(1)} %copy-done.76, f32[16,128,128]{2,1,0:T(8,128)} %fusion.217, ...), kind=kOutput, calls=%fused_computation.53 | convolution fusion | flops 2484502528 | bytes 29966336 | tf_op jit(solution)/shard_map/transpose(jvp(vmap(kijh,kjhp->kihp)))/dot_general | solution.py:42
  1011.9 8.9 rev.44
  1050.2 14.3 multiply_reduce_fusion.4
  1064.7 9.3 broadcast_multiply_fusion
  1085.4 9.3 fusion.84
  1107.0 8.5 add_bitcast_fusion
  1116.8 7.2 convolution_bitcast_fusion
  1130.3 7.0 fusion.90
  1137.4 8.0 fusion.92
  1145.4 64.2 %reduce-scatter.12.cloned.1.call-done = f32[1,1024,768]{2,1,0:T(8,128)} async-done(((f32[1,2048,768]{2,1,0:T(8,128)}), f32[1,1024,768]{2,1,0:T(8,128)}) %reduce-scatter.12.cloned.1.call-update) | async-done | bytes 3145744 | tf_op jit(solution)/shard_map/reduce_scatter | solution.py:237
  1215.2 73.9 %reduce-scatter.10.cloned.1.call-done = f32[1,1024,768]{2,1,0:T(8,128)} async-done(((f32[1,2048,768]{2,1,0:T(8,128)}), f32[1,1024,768]{2,1,0:T(8,128)}) %reduce-scatter.10.cloned.1.call-update) | async-done | bytes 3145744 | tf_op jit(solution)/shard_map/reduce_scatter | solution.py:211
  1299.5 11.3 reduce.61
  1318.1 7.1 fusion.85
  1329.2 11.5 reduce.60
  1342.1 9.3 all-to-all-done.3
  1351.4 9.8 all-to-all-start.1
  1362.8 102.5 %all-reduce.35.cloned.1.call-done = f32[768,128]{1,0:T(8,128)} async-done(((f32[768,128]{1,0:T(8,128)}), f32[768,128]{1,0:T(8,128)}) %all-reduce.35.cloned.1.call-update) | async-done | bytes 393232 | tf_op jit(solution)/shard_map/psum | solution.py:14
  1471.7 58.2 %all-reduce.28 = (f32[768]{0:T(1024)}, f32[4,768]{1,0:T(4,128)}, f32[4,128]{1,0:T(4,128)}, f32[24]{0:T(128)}, f32[12]{0:T(128)}, /*index=5*/f32[12]{0:T(128)}, f32[768]{0:T(1024)}) all-reduce(f32[768]{0:T(1024)S(1)} %get-tuple-element.843, f32[4,768]{1,0:T(4,128)S(1)} %pad_add_fusion.7, ...), channel_id=1, replica_groups=mesh['dp'=16,'tensor'=2] {'dp'}, use_global_device_ids=true, to_apply=%region_38.39 | all-reduce | flops 5168 | bytes 41344 | tf_op jit(solution)/shard_map/psum | solution.py:14
  1539.5 10.0 reshape.1526
  1552.9 45.7 %reduce-scatter.16.cloned.1.call-done = f32[48,768]{1,0:T(8,128)} async-done(((f32[768,768]{1,0:T(8,128)}), f32[48,768]{1,0:T(8,128)}) %reduce-scatter.16.cloned.1.call-update) | async-done | bytes 147472 | tf_op jit(solution)/shard_map/reduce_scatter | solution.py:252
  1598.5 66.3 %reduce-scatter.20.cloned.1.call-done = f32[768,48]{0,1:T(8,128)} async-done(((f32[768,768]{0,1:T(8,128)}), f32[768,48]{0,1:T(8,128)}) %reduce-scatter.20.cloned.1.call-update) | async-done | bytes 147472 | tf_op jit(solution)/shard_map/reduce_scatter | solution.py:255
  (876 shorter events, 498.0 us)
Async XLA Ops:
  7.2 46.7 %copy-start.92 = (f32[768]{0:T(1024)S(1)}, f32[768]{0:T(1024)}, u32[]{:S(2)}) copy-start(f32[768]{0:T(1024)} %param.28) | copy-start | bytes 9220
  7.2 133.0 %all-gather.7.cloned.1.call-start = ((), (), s32[]{:S(2)}) async-start(), calls=%async_computation.11 | async-start | bytes 4718592 | tf_op jit(solution)/shard_map/all_gather | solution.py:153
  53.4 52.2 %copy-start.135 = (f32[12]{0:T(128)S(1)}, f32[12]{0:T(128)}, u32[]{:S(2)}) copy-start(f32[12]{0:T(128)} %param.36) | copy-start | bytes 148
  53.4 52.3 %copy-start.123 = (f32[768]{0:T(1024)S(1)}, f32[768]{0:T(1024)}, u32[]{:S(2)}) copy-start(f32[768]{0:T(1024)} %param.38) | copy-start | bytes 9220
  53.4 52.9 %copy-start.134 = (s32[16]{0:T(128)S(1)}, s32[16]{0:T(128)}, u32[]{:S(2)}) copy-start(s32[16]{0:T(128)} %param.26) | copy-start | bytes 196
  53.4 54.2 %copy-start.112 = (bf16[48,128]{1,0:T(8,128)(2,1)S(1)}, bf16[48,128]{1,0:T(8,128)(2,1)}, u32[]{:S(2)}) copy-start(bf16[48,128]{1,0:T(8,128)(2,1)} %param.31) | copy-start | bytes 36868
  53.8 80.7 %copy-start.113 = (f32[4,768]{1,0:T(4,128)S(1)}, f32[4,768]{1,0:T(4,128)}, u32[]{:S(2)}) copy-start(f32[4,768]{1,0:T(4,128)} %param.33) | copy-start | bytes 36868
  53.8 81.3 %copy-start.129 = (f32[4,128]{1,0:T(4,128)S(1)}, f32[4,128]{1,0:T(4,128)}, u32[]{:S(2)}) copy-start(f32[4,128]{1,0:T(4,128)} %param.34) | copy-start | bytes 6148
  53.9 79.9 %copy-start.94 = (f32[1024]{0:T(1024)}, f32[1024]{0:T(1024)S(1)}, u32[]{:S(2)}) copy-start(f32[1024]{0:T(1024)S(1)} %rsqrt.24) | copy-start | bytes 12292
  56.5 83.7 %copy-start.130 = (f32[24]{0:T(128)S(1)}, f32[24]{0:T(128)}, u32[]{:S(2)}) copy-start(f32[24]{0:T(128)} %param.35) | copy-start | bytes 292
  56.5 120.0 %all-gather.9.cloned.1.call-start = ((), (), s32[]{:S(2)}) async-start(), calls=%async_computation.12 | async-start | bytes 1253376 | tf_op jit(solution)/shard_map/all_gather | solution.py:156
  57.3 488.9 %all-gather.11.cloned.1.call-start = ((), (), s32[]{:S(2)}) async-start(), calls=%async_computation.13 | async-start | bytes 1253376 | tf_op jit(solution)/shard_map/all_gather | solution.py:155
  58.0 77.6 %all-to-all-start.2 = ((bf16[16,1,64,768]{3,2,1,0:T(8,128)(2,1)}), bf16[16,1,64,768]{3,2,1,0:T(8,128)(2,1)}, u32[]{:S(2)}, u32[]{:S(2)}) async-start(bf16[16,1,64,768]{3,2,1,0:T(8,128)(2,1)} %param.25), calls=%async_computation.3 | async-start | bytes 3145728 | tf_op jit(solution)/shard_map/all_to_all | solution.py:139
  63.1 502.1 %all-gather.13.cloned.1.call-start = ((), (), s32[]{:S(2)}) async-start(), calls=%async_computation.14 | async-start | bytes 1253376 | tf_op jit(solution)/shard_map/all_gather | solution.py:159
  63.7 501.6 %all-gather.15.cloned.1.call-start = ((), (), s32[]{:S(2)}) async-start(), calls=%async_computation.16 | async-start | bytes 4718592 | tf_op jit(solution)/shard_map/all_gather | solution.py:207
  105.7 38.1 %copy-start.71 = (bf16[768,24]{0,1:T(8,128)(2,1)}, bf16[768,24]{0,1:T(8,128)(2,1)S(1)}, u32[]{:S(2)}) copy-start(bf16[768,24]{0,1:T(8,128)(2,1)S(1)} %reshape.1504) | copy-start | bytes 110596
  105.7 38.2 %copy-start.126 = (f32[12]{0:T(128)}, f32[12]{0:T(128)S(1)}, u32[]{:S(2)}) copy-start(f32[12]{0:T(128)S(1)} %exp.196) | copy-start | bytes 148
  133.9 42.5 %copy-start.85 = (f32[2048]{0:T(1024)}, f32[2048]{0:T(1024)S(1)}, u32[]{:S(2)}) copy-start(f32[2048]{0:T(1024)S(1)} %fusion.193) | copy-start | bytes 24580
  138.6 966.0 %reduce-scatter.14.cloned.1.call-start = ((), (), s32[]{:S(2)}) async-start(), calls=%async_computation.18 | async-start | bytes 1572864 | tf_op jit(solution)/shard_map/reduce_scatter | solution.py:238
  169.6 32.4 %copy-start.87 = (f32[16,12]{1,0:T(8,128)}, f32[16,12]{1,0:T(8,128)S(1)}, u32[]{:S(2)}) copy-start(f32[16,12]{1,0:T(8,128)S(1)} %get-tuple-element.878) | copy-start | bytes 2308
  176.4 138.3 %copy-start.56 = (f32[2048,12]{0,1:T(8,128)}, f32[2048,12]{0,1:T(8,128)S(1)}, u32[]{:S(2)}) copy-start(f32[2048,12]{0,1:T(8,128)S(1)} %get-tuple-element.885) | copy-start | bytes 294916
  176.5 37.1 %copy-start.63 = (f32[16,128,12]{1,0,2:T(8,128)}, f32[16,128,12]{1,0,2:T(8,128)S(1)}, u32[]{:S(2)}) copy-start(f32[16,128,12]{1,0,2:T(8,128)S(1)} %slice_bitcast_fusion.3) | copy-start | bytes 294916
  418.9 14.9 copy-start.110
  432.1 31.5 %copy-start.54 = (f32[16,128,12]{1,2,0:T(8,128)}, f32[16,128,12]{1,2,0:T(8,128)S(1)}, u32[]{:S(2)}) copy-start(f32[16,128,12]{1,2,0:T(8,128)S(1)} %copy.646) | copy-start | bytes 294916
  433.8 29.8 %copy-start.75 = (f32[16,128,12]{1,2,0:T(8,128)}, f32[16,128,12]{1,2,0:T(8,128)S(1)}, u32[]{:S(2)}) copy-start(f32[16,128,12]{1,2,0:T(8,128)S(1)} %copy.636) | copy-start | bytes 294916
  433.8 29.8 %copy-start.21 = (f32[16,128,768]{1,2,0:S(1)}, f32[16,128,768]{1,2,0}, u32[]{:S(2)}) copy-start(f32[16,128,768]{1,2,0} %fusion.216) | copy-start | bytes 18874372
  433.8 29.8 %copy-start.53 = (f32[16,128,12]{1,2,0:T(8,128)S(1)}, f32[16,128,12]{1,2,0:T(8,128)}, u32[]{:S(2)}) copy-start(f32[16,128,12]{1,2,0:T(8,128)} %copy.628) | copy-start | bytes 294916
  433.8 29.8 %copy-start.60 = (f32[16,128,128]{2,1,0:T(8,128)S(1)}, f32[16,128,128]{2,1,0:T(8,128)}, u32[]{:S(2)}) copy-start(f32[16,128,128]{2,1,0:T(8,128)} %fusion.215) | copy-start | bytes 3145732
  433.8 29.8 %copy-start.73 = (f32[16,128,12]{1,2,0:T(8,128)S(1)}, f32[16,128,12]{1,2,0:T(8,128)}, u32[]{:S(2)}) copy-start(f32[16,128,12]{1,2,0:T(8,128)} %copy.618) | copy-start | bytes 294916
  463.7 29.3 %copy-start.64 = (f32[16,128,12]{1,0,2:T(8,128)S(1)}, f32[16,128,12]{1,0,2:T(8,128)}, u32[]{:S(2)}) copy-start(f32[16,128,12]{1,0,2:T(8,128)} %copy-done.63) | copy-start | bytes 294916
  693.0 28.0 %slice-start.2 = ((s8[6291456]{0:T(1024)(128)(4,1)}), s8[4194304]{0:T(1024)(128)(4,1)S(1)}, s32[]{:S(2)}) async-start(s8[6291456]{0:T(1024)(128)(4,1)} %bitcast.601), calls=%async_computation.27 | async-start | bytes 8388608
  829.8 34.4 %slice-start = ((s8[6291456]{0:T(1024)(128)(4,1)}), s8[2097152]{0:T(1024)(128)(4,1)S(1)}, s32[]{:S(2)}) async-start(s8[6291456]{0:T(1024)(128)(4,1)} %bitcast.584), calls=%async_computation.25 | async-start | bytes 4194304
  829.8 34.4 %slice-start.4 = ((s8[6291456]{0:T(1024)(128)(4,1)}), s8[4194304]{0:T(1024)(128)(4,1)S(1)}, s32[]{:S(2)}) async-start(s8[6291456]{0:T(1024)(128)(4,1)} %bitcast.650), calls=%async_computation.29 | async-start | bytes 8388608
  829.8 34.4 %slice-start.6 = ((s8[6291456]{0:T(1024)(128)(4,1)}), s8[4194304]{0:T(1024)(128)(4,1)S(1)}, s32[]{:S(2)}) async-start(s8[6291456]{0:T(1024)(128)(4,1)} %bitcast.654), calls=%async_computation.31 | async-start | bytes 8388608
  837.0 27.2 %slice-start.1 = ((s8[6291456]{0:T(1024)(128)(4,1)}), s8[4194304]{0:T(1024)(128)(4,1)S(1)}, s32[]{:S(2)}) async-start(s8[6291456]{0:T(1024)(128)(4,1)} %bitcast.584), calls=%async_computation.26 | async-start | bytes 8388608
  837.0 27.2 %slice-start.5 = ((s8[6291456]{0:T(1024)(128)(4,1)}), s8[2097152]{0:T(1024)(128)(4,1)S(1)}, s32[]{:S(2)}) async-start(s8[6291456]{0:T(1024)(128)(4,1)} %bitcast.650), calls=%async_computation.30 | async-start | bytes 4194304
  837.0 27.2 %slice-start.7 = ((s8[6291456]{0:T(1024)(128)(4,1)}), s8[2097152]{0:T(1024)(128)(4,1)S(1)}, s32[]{:S(2)}) async-start(s8[6291456]{0:T(1024)(128)(4,1)} %bitcast.654), calls=%async_computation.32 | async-start | bytes 4194304
  837.0 27.2 %copy-start.61 = (f32[16,128,128]{2,1,0:T(8,128)S(1)}, f32[16,128,128]{2,1,0:T(8,128)}, u32[]{:S(2)}) copy-start(f32[16,128,128]{2,1,0:T(8,128)} %fusion.215) | copy-start | bytes 3145732
  837.1 27.2 %copy-start.74 = (f32[16,128,12]{1,2,0:T(8,128)S(1)}, f32[16,128,12]{1,2,0:T(8,128)}, u32[]{:S(2)}) copy-start(f32[16,128,12]{1,2,0:T(8,128)} %copy.618) | copy-start | bytes 294916
  837.1 27.2 %copy-start.82 = (f32[16,128,12]{1,2,0:T(8,128)S(1)}, f32[16,128,12]{1,2,0:T(8,128)}, u32[]{:S(2)}) copy-start(f32[16,128,12]{1,2,0:T(8,128)} %copy.691) | copy-start | bytes 294916
  837.1 27.2 %copy-start.83 = (f32[16,128,12]{1,2,0:T(8,128)S(1)}, f32[16,128,12]{1,2,0:T(8,128)}, u32[]{:S(2)}) copy-start(f32[16,128,12]{1,2,0:T(8,128)} %copy.666) | copy-start | bytes 294916
  956.8 42.9 %copy-start.45 = (f32[16,128,64]{1,2,0:T(8,128)S(1)}, f32[16,128,64]{1,2,0:T(8,128)}, u32[]{:S(2)}) copy-start(f32[16,128,64]{1,2,0:T(8,128)} %fusion.130) | copy-start | bytes 1572868
  998.7 22.2 %copy-start.46 = (f32[1,16,128,64]{2,3,1,0:T(8,128)S(1)}, f32[1,16,128,64]{2,3,1,0:T(8,128)}, u32[]{:S(2)}) copy-start(f32[1,16,128,64]{2,3,1,0:T(8,128)} %fusion.137) | copy-start | bytes 1572868
  1002.5 18.3 %copy-start.32 = (f32[16,128,128]{2,1,0:T(8,128)S(1)}, f32[16,128,128]{2,1,0:T(8,128)}, u32[]{:S(2)}) copy-start(f32[16,128,128]{2,1,0:T(8,128)} %copy-done.31) | copy-start | bytes 3145732
  1002.5 23.4 %copy-start.47 = (f32[1,16,128,64]{2,3,1,0:T(8,128)S(1)}, f32[1,16,128,64]{2,3,1,0:T(8,128)}, u32[]{:S(2)}) copy-start(f32[1,16,128,64]{2,3,1,0:T(8,128)} %fusion.132) | copy-start | bytes 1572868
  1041.3 89.0 %all-reduce.33.cloned.1.call-start = ((), (), s32[]{:S(2)}) async-start(), calls=%async_computation.21 | async-start | bytes 786432 | tf_op jit(solution)/shard_map/psum | solution.py:14
  1107.0 102.7 %reduce-scatter.12.cloned.1.call-start = ((), (), s32[]{:S(2)}) async-start(), calls=%async_computation.17 | async-start | bytes 9437184 | tf_op jit(solution)/shard_map/reduce_scatter | solution.py:237
  1115.5 173.6 %reduce-scatter.10.cloned.1.call-start = ((), (), s32[]{:S(2)}) async-start(), calls=%async_computation.15 | async-start | bytes 9437184 | tf_op jit(solution)/shard_map/reduce_scatter | solution.py:211
  1124.0 237.4 %reduce-scatter.22.cloned.1.call-start = ((), (), s32[]{:S(2)}) async-start(), calls=%async_computation.24 | async-start | bytes 417792
  1127.8 337.5 %all-reduce.35.cloned.1.call-start = ((), (), s32[]{:S(2)}) async-start(), calls=%async_computation.22 | async-start | bytes 786432 | tf_op jit(solution)/shard_map/psum | solution.py:14
  1130.3 422.6 %reduce-scatter.18.cloned.1.call-start = ((), (), s32[]{:S(2)}) async-start(), calls=%async_computation.20 | async-start | bytes 2506752 | tf_op jit(solution)/shard_map/reduce_scatter | solution.py:253
  1137.3 72.3 %copy-start.44 = (f32[1,1024,128]{2,1,0:T(8,128)S(1)}, f32[1,1024,128]{2,1,0:T(8,128)}, u32[]{:S(2)}) copy-start(f32[1,1024,128]{2,1,0:T(8,128)} %reduce-scatter.14.cloned.1.call-done) | copy-start | bytes 1572868
  1137.3 72.3 %copy-start.49 = (bf16[768,128]{1,0:T(8,128)(2,1)S(1)}, bf16[768,128]{1,0:T(8,128)(2,1)}, u32[]{:S(2)}) copy-start(bf16[768,128]{1,0:T(8,128)(2,1)} %all_gather.24) | copy-start | bytes 589828
  1137.3 72.3 %copy-start.93 = (f32[768]{0:T(1024)S(1)}, f32[768]{0:T(1024)}, u32[]{:S(2)}) copy-start(f32[768]{0:T(1024)} %param.28) | copy-start | bytes 9220
  1137.4 72.3 %copy-start.95 = (f32[1024]{0:T(1024)S(1)}, f32[1024]{0:T(1024)}, u32[]{:S(2)}) copy-start(f32[1024]{0:T(1024)} %copy-done.94) | copy-start | bytes 12292
  1137.4 461.2 %reduce-scatter.16.cloned.1.call-start = ((), (), s32[]{:S(2)}) async-start(), calls=%async_computation.19 | async-start | bytes 2506752 | tf_op jit(solution)/shard_map/reduce_scatter | solution.py:252
  1145.4 143.7 %copy-start.97 = (f32[1,1024]{1,0:T(1,128)S(1)}, f32[1,1024]{1,0:T(1,128)}, u32[]{:S(2)}) copy-start(f32[1,1024]{1,0:T(1,128)} %copy-done.96) | copy-start | bytes 12292
  1312.2 39.2 %all-to-all-start.3 = ((bf16[16,2,24576]{2,1,0:T(2,128)(2,1)}), bf16[16,2,24576]{2,1,0:T(2,128)(2,1)S(1)}, u32[]{:S(2)}, u32[]{:S(2)}) async-start(bf16[16,2,24576]{2,1,0:T(2,128)(2,1)} %reshape.1527), calls=%async_computation.6 | async-start | bytes 3145728 | tf_op jit(solution)/shard_map/all_to_all | solution.py:268
  1317.8 347.0 %reduce-scatter.20.cloned.1.call-start = ((), (), s32[]{:S(2)}) async-start(), calls=%async_computation.23 | async-start | bytes 2506752 | tf_op jit(solution)/shard_map/reduce_scatter | solution.py:255
  1329.2 32.0 %copy-start.106 = (f32[12,64]{1,0:T(8,128)S(1)}, f32[12,64]{1,0:T(8,128)}, u32[]{:S(2)}) copy-start(f32[12,64]{1,0:T(8,128)} %get-tuple-element.761) | copy-start | bytes 9220
  1329.2 32.1 %copy-start.136 = (f32[12]{0:T(128)S(1)}, f32[12]{0:T(128)}, u32[]{:S(2)}) copy-start(f32[12]{0:T(128)} %param.36) | copy-start | bytes 148
  1329.2 142.4 %copy-start.128 = (f32[12]{0:T(128)S(1)}, f32[12]{0:T(128)}, u32[]{:S(2)}) copy-start(f32[12]{0:T(128)} %get-tuple-element.768) | copy-start | bytes 148
  1351.4 188.1 %all-to-all-start.1 = ((bf16[16,2,24576]{2,1,0:T(2,128)(2,1)}), bf16[16,2,24576]{2,1,0:T(2,128)(2,1)}, u32[]{:S(2)}, u32[]{:S(2)}) async-start(bf16[16,2,24576]{2,1,0:T(2,128)(2,1)} %reshape.1525), calls=%async_computation.2 | async-start | bytes 3145728 | tf_op jit(solution)/shard_map/all_to_all | solution.py:265
  1536.1 128.7 %copy-start.1 = (bf16[16,1,64,768]{3,2,1,0:T(8,128)(2,1)S(1)}, bf16[16,1,64,768]{3,2,1,0:T(8,128)(2,1)}, u32[]{:S(2)}) copy-start(bf16[16,1,64,768]{3,2,1,0:T(8,128)(2,1)} %param.24) | copy-start | bytes 4718596
  (98 other events, 743.0 us)
Sparse Core Ops, SparseCore 0:
  56.7 45.2 all-gather.6
  104.3 38.4 all-gather.8
  145.1 37.1 all-gather.10
  184.5 37.2 all-gather.12
  223.7 43.8 all-gather.14
  1041.4 17.7 reduce-scatter.13
  1107.1 23.1 all-reduce.32
  1132.6 77.0 reduce-scatter.11
  1212.1 77.0 reduce-scatter.9
  1292.5 67.6 reduce-scatter.21
  1363.9 101.3 all-reduce.34
  1469.5 62.2 reduce-scatter.17
  1536.7 61.8 reduce-scatter.15
  1602.7 62.0 reduce-scatter.19
